TPU v7x, 256 devices: a whole 4x4x8 slice. The times are simulated.
256 devices in a mesh: pair: 32 (over y, x, core), win: 8 (over z).
Axes of the slice: x: 4, y: 4, z: 8, core: 2. Of those that a mesh axis runs over, the one named last changes fastest.
Arguments:
- spectra: float32 [2, 8, 6144, 2048], P(None, 'win', 'pair'), may hold values from -400 to 400
- pair_list: int32 [32, 2, 2], replicated, may hold values from 0 to 95, as said below
Outputs:
- stack: float32 [64, 8, 32, 16, 1024], P('pair', 'win')
Inputs may be any that keep to these rules, and one draw needn't show every extreme that they name: For each owner q, the 4 blocks listed in pair_list[q] lie on 4 different indices of pair (block k on index k // 3): at most one from any index.
All inputs are finite; a program needn't handle non-finite values.
Results may differ from a plain program's by a relative error of at most 0.0056.
Values may be sent and summed in bfloat16 or wider, within the bound.
A program may use at most 256 MiB of HBM per device.

v0:
```python
import jax
import jax.numpy as jnp
from jax import lax
from jax.sharding import PartitionSpec as P

CH = 64
NF = 2048
BAND = 128
NLAG = 1024


whiten_eps = 1e-06


def whiten(spectra):
    powers = spectra[0] * spectra[0] + spectra[1] * spectra[1]
    lead = powers.shape[:-1]
    band_power = jnp.mean(powers.reshape(lead + (NF // BAND, BAND)), axis=-1)
    scales = lax.rsqrt(band_power + whiten_eps)
    banded = spectra.reshape((2,) + lead + (NF // BAND, BAND))
    return (banded * scales[None, ..., None]).reshape(spectra.shape).astype(jnp.bfloat16)


def lag_tables(windows):
    half = NLAG // 2
    freqs = jnp.arange(NF, dtype=jnp.int32)
    magnitudes = jnp.arange(1, half + 1, dtype=jnp.int32)
    phases = jnp.mod(freqs[:, None] * magnitudes[None, :], 2 * NF)
    angles = phases.astype(jnp.float32) * (jnp.pi / NF)
    weights = jnp.where(freqs == 0, 1.0, 2.0).astype(jnp.float32) / jnp.sqrt(
        jnp.float32(NF * windows)
    )
    cos_pos = (weights[:, None] * jnp.cos(angles)).astype(jnp.bfloat16)
    sin_pos = ((-weights)[:, None] * jnp.sin(angles)).astype(jnp.bfloat16)
    return (cos_pos, sin_pos, weights.astype(jnp.bfloat16))


def cross_spectra(incoming, source_device, receiver_device):
    bins = incoming.shape[-1]
    source = jnp.take(incoming, source_device, axis=2)
    receiver = jnp.take(incoming, receiver_device, axis=2)
    win_here = source.shape[1]
    slot_count = source.shape[2]
    win_devices = lax.axis_size("win")
    half_span = win_devices // 2
    src_tile = CH // 2
    rcv_tile = CH // half_span
    src_split = source.reshape(2, win_here, slot_count, 2, src_tile, bins)
    rcv_split = receiver.reshape(2, win_here, slot_count, half_span, rcv_tile, bins)
    src_out = jnp.repeat(src_split, half_span, axis=3)
    rcv_out = jnp.concatenate([rcv_split, rcv_split], axis=3)
    src_all, rcv_all = (
        lax.all_to_all(src_out, "win", split_axis=3, concat_axis=1, tiled=True),
        lax.all_to_all(rcv_out, "win", split_axis=3, concat_axis=1, tiled=True),
    )
    src_one = src_all[:, :, :, 0]
    rcv_one = rcv_all[:, :, :, 0]
    real_part = jnp.einsum(
        "wiaf,wibf->iabf", src_one[0], rcv_one[0], preferred_element_type=jnp.float32
    )
    real_part = real_part + jnp.einsum(
        "wiaf,wibf->iabf", src_one[1], rcv_one[1], preferred_element_type=jnp.float32
    )
    imag_part = jnp.einsum(
        "wiaf,wibf->iabf", src_one[1], rcv_one[0], preferred_element_type=jnp.float32
    )
    imag_part = imag_part - jnp.einsum(
        "wiaf,wibf->iabf", src_one[0], rcv_one[1], preferred_element_type=jnp.float32
    )
    return (real_part.astype(jnp.bfloat16), imag_part.astype(jnp.bfloat16))


def body(spectra, pair_list):
    white = whiten(spectra)
    win_here = white.shape[1]
    block_count = white.shape[2] // CH
    blocks = white.reshape(2, win_here, block_count, CH, NF)
    pair_devices = lax.axis_size("pair")
    my_index = lax.axis_index("pair")
    endpoints = pair_list.reshape(pair_devices, -1)
    on_device = endpoints // block_count == my_index
    local_block = jnp.sum(jnp.where(on_device, endpoints % block_count, 0), axis=1)
    present = jnp.any(on_device, axis=1)
    picked = jnp.take(blocks, local_block, axis=2)
    outgoing = jnp.where(present[None, None, :, None, None], picked, jnp.zeros_like(picked))
    my_pairs = lax.dynamic_index_in_dim(pair_list, my_index, 0, keepdims=False)
    source_device = my_pairs[:, 0] // block_count
    receiver_device = my_pairs[:, 1] // block_count
    incoming = lax.all_to_all(outgoing, "pair", split_axis=2, concat_axis=2, tiled=True)
    rounded_re, rounded_im = cross_spectra(incoming, source_device, receiver_device)
    slot_count = rounded_re.shape[0]
    src_tile = rounded_re.shape[1]
    rcv_tile = rounded_re.shape[2]
    windows = win_here * lax.axis_size("win")
    cos_pos, sin_pos, centre_weights = lag_tables(windows)
    half = NLAG // 2
    flat_re = rounded_re.reshape(-1, NF)
    flat_im = rounded_im.reshape(-1, NF)
    cos_part = jnp.dot(flat_re, cos_pos, preferred_element_type=jnp.float32)
    sin_part = jnp.dot(flat_im, sin_pos, preferred_element_type=jnp.float32)
    centre = jnp.dot(flat_re, centre_weights, preferred_element_type=jnp.float32)
    lagged = jnp.concatenate(
        [(cos_part - sin_part)[:, ::-1], centre[:, None], (cos_part + sin_part)[:, : half - 1]],
        axis=1,
    )
    return lagged.reshape(slot_count, 1, src_tile, rcv_tile, NLAG)


def solution(mesh):
    in_specs = (P(None, "win", "pair", None), P())
    out_specs = P("pair", "win", None, None, None)
    return jax.shard_map(body, mesh=mesh, in_specs=in_specs, out_specs=out_specs, check_vma=False)
```

profile of v0, /device:TPU:6, one launch (start us, length us, event | category | flops | bytes accessed | tf_op | source)
XLA Modules:
  0.0 632.1 jit_solution(11178866883825231688)
XLA Ops:
  0.0 0.7 fusion.33
  0.7 0.7 fusion.23
  1.4 2.1 add_bitcast_fusion
  5.0 0.6 copy.85
  5.6 2.4 multiply_convert_fusion.2
  8.0 7.0 %gather_fusion = bf16[32,2,64,2048]{3,2,1,0:T(8,128)(2,1)} fusion(bf16[2,3,64,2048]{3,2,1,0:T(8,128)(2,1)S(1)} %bitcast.92, s32[1024]{0:T(1024)S(1)} %pad_clamp_fusion.2), kind=kCustom, calls=%fused_computation.2 | custom fusion | bytes 33554560 | tf_op jit(solution)/shard_map/jit(_take)/gather | solution.py:84
  15.0 14.3 %fusion.1 = bf16[2,1,32,64,2048]{4,3,0,1,2:T(8,128)(2,1)} fusion(bf16[32,2,64,2048]{3,2,1,0:T(8,128)(2,1)} %gather_fusion, pred[32]{0:T(512)(128)(4,1)S(1)} %compare_and_fusion.2, pred[32]{0:T(512)(128)(4,1)S(1)} %get-tuple-element.14), kind=kLoop, calls=%fused_computation.7 | loop fusion | flops 16777216 | bytes 33554496 | tf_op jit(solution)/shard_map/jit(_where)/select_n | solution.py:85
  29.2 7.9 %all-to-all-start = ((bf16[2,1,32,64,2048]{4,3,0,1,2:T(8,128)(2,1)}), bf16[2,1,32,64,2048]{4,3,0,1,2:T(8,128)(2,1)}, u32[]{:S(2)}, u32[]{:S(2)}) async-start(bf16[2,1,32,64,2048]{4,3,0,1,2:T(8,128)(2,1)} %fusion.1), calls=%async_computation | async-start | bytes 33554432 | tf_op jit(solution)/shard_map/all_to_all | solution.py:89
  37.8 203.4 %all-to-all-done = bf16[2,1,32,64,2048]{4,3,0,1,2:T(8,128)(2,1)} async-done(((bf16[2,1,32,64,2048]{4,3,0,1,2:T(8,128)(2,1)}), bf16[2,1,32,64,2048]{4,3,0,1,2:T(8,128)(2,1)}, u32[]{:S(2)}, u32[]{:S(2)}) %all-to-all-start) | async-done | bytes 16777248 | tf_op jit(solution)/shard_map/all_to_all | solution.py:89
  241.2 14.1 %copy.84 = bf16[2,1,32,64,2048]{4,3,2,0,1:T(8,128)(2,1)} copy(bf16[2,1,32,64,2048]{4,3,0,1,2:T(8,128)(2,1)} %all-to-all-done) | data formatting | bytes 33554432 | tf_op jit(solution)/shard_map/all_to_all | solution.py:89
  255.3 6.4 %gather_fusion.1 = bf16[2,2,64,2048]{3,2,1,0:T(8,128)(2,1)S(1)} fusion(bf16[2,32,64,2048]{3,2,1,0:T(8,128)(2,1)} %bitcast.93, s32[1024]{0:T(1024)S(1)} %pad_clamp_fusion.1), kind=kCustom, calls=%fused_computation.clone | custom fusion | bytes 2097160 | tf_op jit(solution)/shard_map/jit(_take)/gather | solution.py:41
  262.1 1.6 copy.69
  263.6 8.5 %all-to-all-start.1 = ((bf16[2,1,2,8,16,2048]{5,4,2,1,0,3:T(8,128)(2,1)}), bf16[2,1,2,8,16,2048]{5,4,2,1,0,3:T(8,128)(2,1)S(1)}, u32[]{:S(2)}, u32[]{:S(2)}) async-start(bf16[2,1,2,8,16,2048]{5,4,2,1,0,3:T(8,128)(2,1)} %copy.69), calls=%async_computation.1 | async-start | bytes 4194304 | tf_op jit(solution)/shard_map/all_to_all | solution.py:54
  272.1 6.4 %gather_fusion.2 = bf16[2,2,64,2048]{3,2,1,0:T(8,128)(2,1)S(1)} fusion(bf16[2,32,64,2048]{3,2,0,1:T(8,128)(2,1)} %bitcast.13, s32[1024]{0:T(1024)S(1)} %pad_clamp_fusion), kind=kCustom, calls=%fused_computation.1.clone | custom fusion | bytes 2097160 | tf_op jit(solution)/shard_map/jit(_take)/gather | solution.py:40
  278.8 45.9 %all-to-all-done.1 = bf16[2,1,2,8,16,2048]{5,4,2,1,0,3:T(8,128)(2,1)S(1)} async-done(((bf16[2,1,2,8,16,2048]{5,4,2,1,0,3:T(8,128)(2,1)}), bf16[2,1,2,8,16,2048]{5,4,2,1,0,3:T(8,128)(2,1)S(1)}, u32[]{:S(2)}, u32[]{:S(2)}) %all-to-all-start.1) | async-done | bytes 2097184 | tf_op jit(solution)/shard_map/all_to_all | solution.py:54
  324.7 2.5 broadcast_in_dim.56
  327.2 4.7 all-to-all-start.2
  332.0 14.5 %copy.70 = bf16[2,1,2,8,16,2048]{4,3,5,2,0,1:T(8,128)(2,1)} copy(bf16[2,1,2,8,16,2048]{5,4,2,1,0,3:T(8,128)(2,1)S(1)} %all-to-all-done.1) | data formatting | bytes 4194304 | tf_op jit(solution)/shard_map/all_to_all | solution.py:54
  346.5 82.3 %all-to-all-done.2 = bf16[2,1,2,8,32,2048]{5,4,2,1,0,3:T(8,128)(2,1)} async-done(((bf16[2,1,2,8,32,2048]{5,4,2,1,0,3:T(8,128)(2,1)}), bf16[2,1,2,8,32,2048]{5,4,2,1,0,3:T(8,128)(2,1)}, u32[]{:S(2)}, u32[]{:S(2)}) %all-to-all-start.2) | async-done | bytes 4194336 | tf_op jit(solution)/shard_map/all_to_all | solution.py:53
  428.8 17.1 %copy.72 = bf16[2,1,2,8,32,2048]{4,3,5,2,0,1:T(8,128)(2,1)} copy(bf16[2,1,2,8,32,2048]{5,4,2,1,0,3:T(8,128)(2,1)} %all-to-all-done.2) | data formatting | bytes 8388608 | tf_op jit(solution)/shard_map/all_to_all | solution.py:53
  445.9 20.3 %fusion.4 = f32[2,2048,16,32]{3,2,1,0:T(8,128)} fusion(bf16[2,8,1,2,1,16,2048]{5,1,6,3,4,2,0:T(8,128)(2,1)} %bitcast.88, bf16[2,8,1,2,1,32,2048]{5,1,6,3,4,2,0:T(8,128)(2,1)} %bitcast.84), kind=kOutput, calls=%fused_computation.15 | convolution fusion | flops 33554432 | bytes 25165824 | tf_op jit(solution)/shard_map/wiaf,wibf->iabf/dot_general | solution.py:64
  466.2 2.3 copy-done
  468.6 15.2 %fusion.5 = f32[2,2048,16,32]{3,2,1,0:T(8,128)} fusion(bf16[2,8,1,2,1,16,2048]{5,1,6,3,4,2,0:T(8,128)(2,1)} %bitcast.89, bf16[2,8,1,2,1,32,2048]{5,1,6,3,4,2,0:T(8,128)(2,1)S(1)} %bitcast.87), kind=kOutput, calls=%fused_computation.16 | convolution fusion | flops 33554432 | bytes 25165824 | tf_op jit(solution)/shard_map/wiaf,wibf->iabf/dot_general | solution.py:58
  483.7 23.4 %fusion.3 = bf16[2,32,16,2048]{1,2,3,0:T(8,128)(2,1)} fusion(f32[2,2048,16,32]{3,2,1,0:T(8,128)} %fusion.4, bf16[2,8,1,2,1,32,2048]{5,1,6,3,4,2,0:T(8,128)(2,1)} %bitcast.85, bf16[2,8,1,2,1,16,2048]{5,1,6,3,4,2,0:T(8,128)(2,1)} %bitcast.90), kind=kOutput, calls=%fused_computation.10 | convolution fusion | flops 37748736 | bytes 54525952 | tf_op jit(solution)/shard_map/wiaf,wibf->iabf/dot_general | solution.py:67
  507.1 19.8 %copy.74 = bf16[2,32,16,2048]{3,2,1,0:T(8,128)(2,1)} copy(bf16[2,32,16,2048]{1,2,3,0:T(8,128)(2,1)} %fusion.3) | data formatting | bytes 8388608 | tf_op jit(solution)/shard_map/convert_element_type | solution.py:70
  526.9 23.5 %fusion.2 = bf16[2,32,16,2048]{1,2,3,0:T(8,128)(2,1)} fusion(f32[2,2048,16,32]{3,2,1,0:T(8,128)} %fusion.5, bf16[2,8,1,2,1,16,2048]{5,1,6,3,4,2,0:T(8,128)(2,1)} %bitcast.91, bf16[2,8,1,2,1,32,2048]{5,1,6,3,4,2,0:T(8,128)(2,1)} %bitcast.86), kind=kOutput, calls=%fused_computation.9 | convolution fusion | flops 37748736 | bytes 54525952 | tf_op jit(solution)/shard_map/wiaf,wibf->iabf/dot_general | solution.py:61
  550.4 20.0 %copy.73 = bf16[2,32,16,2048]{3,2,1,0:T(8,128)(2,1)} copy(bf16[2,32,16,2048]{1,2,3,0:T(8,128)(2,1)} %fusion.2) | data formatting | bytes 8388608 | tf_op jit(solution)/shard_map/convert_element_type | solution.py:70
  570.4 19.6 %fusion.13 = f32[1024,512]{1,0:T(8,128)S(1)} fusion(bf16[1024,2048]{1,0:T(8,128)(2,1)} %bitcast.101, f32[2048]{0:T(1024)S(1)} %fusion.20, s32[512]{0:T(512)S(1)} %iota_add_fusion), kind=kOutput, calls=%fused_computation.31 | convolution fusion | flops 2164260864 | bytes 6301696 | tf_op jit(solution)/shard_map/dot_general | solution.py:100
  590.0 18.2 %fusion.35 = (f32[1024,512]{1,0:T(8,128)}, f32[1024,512]{1,0:T(8,128)S(1)}) fusion(f32[1024,512]{1,0:T(8,128)S(1)} %fusion.13, bf16[1024,2048]{1,0:T(8,128)(2,1)S(1)} %bitcast.100, s32[512]{0:T(512)S(1)} %iota_add_fusion, f32[2048]{0:T(1024)S(1)} %select_multiply_fusion), kind=kOutput, calls=%fused_computation.81 | convolution fusion | flops 2164785152 | bytes 10496000 | tf_op jit(solution)/shard_map/dot_general | solution.py:99
  608.6 1.2 convolution_bitcast_fusion
  609.9 17.6 %rev.3 = f32[1024,512]{1,0:T(8,128)} reverse(f32[1024,512]{1,0:T(8,128)} %get-tuple-element.16), dimensions={1} | reverse | bytes 4194304 | tf_op jit(solution)/shard_map/rev | solution.py:103
  627.5 4.4 pad_maximum_fusion
  (31 shorter events, 3.2 us)
Async XLA Ops:
  29.2 7.9 %copy-start.2 = (s32[32,2,2]{0,2,1:T(2,128)S(1)}, s32[32,2,2]{0,2,1:T(2,128)}, u32[]{:S(2)}) copy-start(s32[32,2,2]{0,2,1:T(2,128)} %param.5) | copy-start | bytes 1540
  29.2 211.9 %all-to-all-start = ((bf16[2,1,32,64,2048]{4,3,0,1,2:T(8,128)(2,1)}), bf16[2,1,32,64,2048]{4,3,0,1,2:T(8,128)(2,1)}, u32[]{:S(2)}, u32[]{:S(2)}) async-start(bf16[2,1,32,64,2048]{4,3,0,1,2:T(8,128)(2,1)} %fusion.1), calls=%async_computation | async-start | bytes 33554432 | tf_op jit(solution)/shard_map/all_to_all | solution.py:89
  263.6 61.1 %all-to-all-start.1 = ((bf16[2,1,2,8,16,2048]{5,4,2,1,0,3:T(8,128)(2,1)}), bf16[2,1,2,8,16,2048]{5,4,2,1,0,3:T(8,128)(2,1)S(1)}, u32[]{:S(2)}, u32[]{:S(2)}) async-start(bf16[2,1,2,8,16,2048]{5,4,2,1,0,3:T(8,128)(2,1)} %copy.69), calls=%async_computation.1 | async-start | bytes 4194304 | tf_op jit(solution)/shard_map/all_to_all | solution.py:54
  327.2 101.6 %all-to-all-start.2 = ((bf16[2,1,2,8,32,2048]{5,4,2,1,0,3:T(8,128)(2,1)}), bf16[2,1,2,8,32,2048]{5,4,2,1,0,3:T(8,128)(2,1)}, u32[]{:S(2)}, u32[]{:S(2)}) async-start(bf16[2,1,2,8,32,2048]{5,4,2,1,0,3:T(8,128)(2,1)} %bitcast.94), calls=%async_computation.2 | async-start | bytes 8388608 | tf_op jit(solution)/shard_map/all_to_all | solution.py:53
  445.9 22.7 %copy-start = (bf16[2,1,2,8,32,2048]{4,3,5,2,0,1:T(8,128)(2,1)S(1)}, bf16[2,1,2,8,32,2048]{4,3,5,2,0,1:T(8,128)(2,1)}, u32[]{:S(2)}) copy-start(bf16[2,1,2,8,32,2048]{4,3,5,2,0,1:T(8,128)(2,1)} %copy.72) | copy-start | bytes 12582916
  570.4 19.6 %copy-start.1 = (bf16[2,32,16,2048]{3,2,1,0:T(8,128)(2,1)S(1)}, bf16[2,32,16,2048]{3,2,1,0:T(8,128)(2,1)}, u32[]{:S(2)}) copy-start(bf16[2,32,16,2048]{3,2,1,0:T(8,128)(2,1)} %copy.73) | copy-start | bytes 12582916
where the time goes:
time: 640 us; the launch traced here: 632 us
  waiting for transfers between devices  332 us (52%)
  local copies, waits for them, and re-layouts  131 us (20%)
  matrix products  121 us (19%)
  other arithmetic  26.4 us (4%)
  starting transfers between devices  21 us (3%)
    all_to_all x1, waiting for transfers between devices, body(): lax.all_to_all(outgoing, 'pair', split_axis=2, concat_axis=2, tiled=True)  203 us
    all_to_all x1, waiting for transfers between devices, cross_spectra(): lax.all_to_all(src_out, 'win', split_axis=3, concat_axis=1, tiled=True)  82.3 us
    all_to_all x1, waiting for transfers between devices, cross_spectra(): lax.all_to_all(rcv_out, 'win', split_axis=3, concat_axis=1, tiled=True)  45.9 us
    convert_element_type x2, local copies, waits for them, and re-layouts, cross_spectra(): return (real_part.astype(jnp.bfloat16), imag_part.astype(jnp.bfloat16))  39.8 us
    dot_general x1, matrix products, cross_spectra(): jnp.einsum('wiaf,wibf->iabf', src_one[1], rcv_one[1], preferred_element_t...  23.5 us
    dot_general x1, matrix products, cross_spectra(): jnp.einsum('wiaf,wibf->iabf', src_one[0], rcv_one[1], preferred_element_t...  23.4 us
    dot_general x1, matrix products, cross_spectra(): jnp.einsum('wiaf,wibf->iabf', src_one[1], rcv_one[0], preferred_element_t...  20.3 us
    dot_general x1, matrix products, body(): sin_part = jnp.dot(flat_im, sin_pos, preferred_element_type=jnp.float32)  19.6 us
  transfers between devices with their start and end apart: 3, of which 3 were waited for; matrix products, arithmetic and copies ran while one was open for 3% of the time, Pallas kernels for 0%

commit v1 on v0

v1 whole, which is shorter than its diff:
```python
import functools

import jax
import jax.numpy as jnp
import ml_dtypes
import numpy as np
from jax import lax
from jax.experimental import pallas as pl
from jax.experimental.pallas import tpu as pltpu
from jax.sharding import PartitionSpec as P

CH = 64
BLK = 3
NF = 2048
BAND = 128
BANDS = NF // BAND
NLAG = 1024
WIN = 8
PAIR = 32
SLOTS = 2
SRC = 32
RCV = 16
PIECES = 2 * BANDS
MESH = pl.DeviceIdType.MESH

whiten_eps = 1e-06


def lag_table():
    freqs = np.arange(NF, dtype=np.int64)
    offsets = np.arange(NLAG, dtype=np.int64) - NLAG // 2
    phases = np.mod(freqs[:, None] * np.abs(offsets)[None, :], 2 * NF)
    angles = phases.astype(np.float32) * np.float32(np.pi / NF)
    weights = np.where(freqs == 0, 1.0, 2.0).astype(np.float32) / np.sqrt(np.float32(NF * WIN))
    cos_table = weights[:, None] * np.cos(angles)
    sin_table = -weights[:, None] * (np.sign(offsets).astype(np.float32)[None, :] * np.sin(angles))
    return np.concatenate([cos_table, sin_table], axis=0).astype(ml_dtypes.bfloat16)


def peer_of(me, step):
    y = lax.rem(me // 8 + step // 8, 4)
    x = lax.rem(lax.rem(me // 2, 4) + lax.rem(step // 2, 4), 4)
    core = lax.rem(lax.rem(me, 2) + lax.rem(step, 2), 2)
    return (y * 4 + x) * 2 + core


def kernel(
    list_ref, spec_ref, table_ref, out_ref,
    white, all_blocks, outgoing, mine, src_in, rcv_in, src_wide, cross, table, lagged,
    one_send, one_recv, two_send, two_recv, z_send, z_recv, local_sem, table_sem, out_sem,
):
    me = lax.axis_index("pair")
    win = lax.axis_index("win")

    barrier = pltpu.get_barrier_semaphore()

    def greet_pair(step, carry):
        pl.semaphore_signal(barrier, inc=1, device_id=(peer_of(me, step), win), device_id_type=MESH)
        return carry

    def greet_win(step, carry):
        pl.semaphore_signal(barrier, inc=1, device_id=(me, lax.rem(win + step, WIN)), device_id_type=MESH)
        return carry

    lax.fori_loop(1, PAIR, greet_pair, 0)
    lax.fori_loop(1, WIN, greet_win, 0)

    table_copy = pltpu.make_async_copy(table_ref, table, table_sem)
    table_copy.start()

    def whiten(band, carry):
        cols = pl.ds(pl.multiple_of(band * BAND, BAND), BAND)
        re = spec_ref[0, 0, :, cols]
        im = spec_ref[1, 0, :, cols]
        level = jnp.sum(re * re + im * im, axis=-1, keepdims=True) * (1.0 / BAND)
        scale = lax.rsqrt(level + whiten_eps)
        white[band] = (re * scale).astype(jnp.bfloat16).reshape(BLK, CH, BAND)
        white[BANDS + band] = (im * scale).astype(jnp.bfloat16).reshape(BLK, CH, BAND)
        return carry

    lax.fori_loop(0, BANDS, whiten, 0)

    pl.semaphore_wait(barrier, PAIR - 1 + WIN - 1)

    def send_one(step, carry):
        to = peer_of(me, step)
        pltpu.make_async_remote_copy(
            src_ref=white.at[to],
            dst_ref=all_blocks.at[pl.ds(me * BLK, BLK)],
            send_sem=one_send,
            recv_sem=one_recv,
            device_id=(to, win),
            device_id_type=MESH,
        ).start()
        return carry

    lax.fori_loop(1, PAIR, send_one, 0)
    all_blocks[pl.ds(me * BLK, BLK)] = white[me]

    most = all_blocks.at[pl.ds(0, (PAIR - 1) * BLK)]
    pltpu.make_async_copy(most, most, one_recv).wait()

    for slot in range(SLOTS):
        def send_two(step, carry):
            to = peer_of(me, step)
            for end in range(2):
                outgoing[to, slot, end] = all_blocks[list_ref[to * 4 + slot * 2 + end]]
            pltpu.make_async_remote_copy(
                src_ref=outgoing.at[to, slot],
                dst_ref=mine.at[slot, me],
                send_sem=two_send.at[slot],
                recv_sem=two_recv.at[slot],
                device_id=(to, win),
                device_id_type=MESH,
            ).start()
            return carry

        lax.fori_loop(1, PAIR, send_two, 0)
        for end in range(2):
            mine[slot, me, end] = all_blocks[list_ref[me * 4 + slot * 2 + end]]

    for slot in range(SLOTS):
        most = mine.at[slot, pl.ds(0, PAIR - 1)]
        pltpu.make_async_copy(most, most, two_recv.at[slot]).wait()

        def views(to):
            src = mine.at[slot, :, 0, pl.ds(pl.multiple_of(to // 4 * SRC, SRC), SRC)]
            rcv = mine.at[slot, :, 1, pl.ds(pl.multiple_of(lax.rem(to, 4) * RCV, RCV), RCV)]
            return src, rcv

        def send_z(step, carry):
            to = lax.rem(win + step, WIN)
            src, rcv = views(to)
            for part, (view, dst) in enumerate(((src, src_in), (rcv, rcv_in))):
                pltpu.make_async_remote_copy(
                    src_ref=view,
                    dst_ref=dst.at[slot, win],
                    send_sem=z_send.at[slot, part],
                    recv_sem=z_recv.at[slot, part],
                    device_id=(me, to),
                    device_id_type=MESH,
                ).start()
            return carry

        lax.fori_loop(1, WIN, send_z, 0)
        src, rcv = views(win)
        pltpu.make_async_copy(src, src_in.at[slot, win], local_sem.at[slot, 0]).start()
        pltpu.make_async_copy(rcv, rcv_in.at[slot, win], local_sem.at[slot, 1]).start()

    table_copy.wait()

    for slot in range(SLOTS):
        src, rcv = src_in.at[slot], rcv_in.at[slot]
        for part, ref in enumerate((src, rcv)):
            most = ref.at[pl.ds(0, WIN - 1)]
            pltpu.make_async_copy(most, most, z_recv.at[slot, part]).wait()
            pltpu.make_async_copy(ref.at[0], ref.at[0], local_sem.at[slot, part]).wait()

        def one_band(band, carry):
            receivers = []
            for w in range(WIN):
                for part in range(2):
                    src_wide[part, w] = src[w, part * BANDS + band].astype(jnp.float32)
                    receivers.append(rcv[w, part * BANDS + band].astype(jnp.float32))

            def one_source(a, inner):
                re = jnp.zeros((RCV, BAND), jnp.float32)
                im = jnp.zeros((RCV, BAND), jnp.float32)
                for w in range(WIN):
                    s_re = jnp.broadcast_to(src_wide[0, w, pl.ds(a, 1), :], (RCV, BAND))
                    s_im = jnp.broadcast_to(src_wide[1, w, pl.ds(a, 1), :], (RCV, BAND))
                    r_re, r_im = receivers[2 * w], receivers[2 * w + 1]
                    re = re + s_re * r_re + s_im * r_im
                    im = im + s_im * r_re - s_re * r_im
                rows = pl.ds(pl.multiple_of(a * RCV, RCV), RCV)
                cross[rows, pl.ds(pl.multiple_of(band * BAND, BAND), BAND)] = re.astype(jnp.bfloat16)
                cross[rows, pl.ds(pl.multiple_of(NF + band * BAND, BAND), BAND)] = im.astype(jnp.bfloat16)
                return inner

            lax.fori_loop(0, SRC, one_source, 0)
            return carry

        lax.fori_loop(0, BANDS, one_band, 0)

        def one_tile(tile, carry):
            cols = pl.ds(pl.multiple_of(tile * 256, 256), 256)
            lagged[slot, :, cols] = jnp.dot(cross[...], table[:, cols], preferred_element_type=jnp.float32)
            return carry

        lax.fori_loop(0, NLAG // 256, one_tile, 0)
        pltpu.make_async_copy(lagged.at[slot], out_ref.at[slot], out_sem.at[slot]).start()

    sent = white.at[pl.ds(0, PAIR - 1)]
    pltpu.make_async_copy(sent, sent, one_send).wait()
    for slot in range(SLOTS):
        sent = outgoing.at[pl.ds(0, PAIR - 1), slot]
        pltpu.make_async_copy(sent, sent, two_send.at[slot]).wait()
        for part, ref in enumerate((src_in, rcv_in)):
            sent = ref.at[slot, pl.ds(0, WIN - 1)]
            pltpu.make_async_copy(sent, sent, z_send.at[slot, part]).wait()
        pltpu.make_async_copy(lagged.at[slot], out_ref.at[slot], out_sem.at[slot]).wait()


def body(spectra, pair_list):
    table = jnp.asarray(lag_table())
    rows = SRC * RCV
    bf16 = jnp.bfloat16
    out = pl.pallas_call(
        kernel,
        out_shape=jax.ShapeDtypeStruct((SLOTS, rows, NLAG), jnp.float32),
        in_specs=[
            pl.BlockSpec(memory_space=pltpu.SMEM),
            pl.BlockSpec(memory_space=pltpu.VMEM),
            pl.BlockSpec(memory_space=pl.ANY),
        ],
        out_specs=pl.BlockSpec(memory_space=pl.ANY),
        scratch_shapes=[
            pltpu.VMEM((PIECES, BLK, CH, BAND), bf16),
            pltpu.VMEM((PAIR * BLK, CH, BAND), bf16),
            pltpu.VMEM((PAIR, SLOTS, 2, CH, BAND), bf16),
            pltpu.VMEM((SLOTS, PIECES, 2, CH, BAND), bf16),
            pltpu.VMEM((SLOTS, WIN, PIECES, SRC, BAND), bf16),
            pltpu.VMEM((SLOTS, WIN, PIECES, RCV, BAND), bf16),
            pltpu.VMEM((2, WIN, SRC, BAND), jnp.float32),
            pltpu.VMEM((rows, 2 * NF), bf16),
            pltpu.VMEM((2 * NF, NLAG), bf16),
            pltpu.VMEM((SLOTS, rows, NLAG), jnp.float32),
            pltpu.SemaphoreType.DMA,
            pltpu.SemaphoreType.DMA,
            pltpu.SemaphoreType.DMA((SLOTS,)),
            pltpu.SemaphoreType.DMA((SLOTS,)),
            pltpu.SemaphoreType.DMA((SLOTS, 2)),
            pltpu.SemaphoreType.DMA((SLOTS, 2)),
            pltpu.SemaphoreType.DMA((SLOTS, 2)),
            pltpu.SemaphoreType.DMA,
            pltpu.SemaphoreType.DMA((SLOTS,)),
        ],
        compiler_params=pltpu.CompilerParams(
            collective_id=0, has_side_effects=True, vmem_limit_bytes=48 * 1024 * 1024
        ),
    )(pair_list.reshape(-1), spectra, table)
    return out.reshape(SLOTS, 1, SRC, RCV, NLAG)


def solution(mesh):
    in_specs = (P(None, "win", "pair", None), P())
    out_specs = P("pair", "win", None, None, None)
    return jax.shard_map(body, mesh=mesh, in_specs=in_specs, out_specs=out_specs, check_vma=False)
```

time: 640 us -> 226 us (0.35)
  the two profiles are of different devices: /device:TPU:6 before, /device:TPU:1 now
where the time goes in v1:
time: 226 us; the launch traced here: 225 us
  Pallas kernels  218 us (96%)
  local copies, waits for them, and re-layouts  7.6 us (3%)
    pallas_call x1, Pallas kernels, body(): pl.pallas_call(kernel, out_shape=jax.ShapeDtypeStruct((SLOTS, rows, NLAG)...  218 us
    unnamed x4, local copies, waits for them, and re-layouts  7.45 us

profile of v1, /device:TPU:1, one launch (start us, length us, event | category | flops | bytes accessed | tf_op | source)
XLA Modules:
  0.0 225.4 jit_solution(15641113206651679455)
XLA Ops:
  0.0 0.8 copy.6
  0.8 0.1 reshape.6.list_ref
  0.9 0.0 copy-start
  0.9 1.9 copy-done
  2.8 217.8 %shard_map.37 = f32[2,512,1024]{2,1,0:T(8,128)} custom-call(s32[128]{0:T(128)S(1)} %reshape.6.list_ref, f32[2,1,192,2048]{3,2,1,0:T(8,128)S(1)} %copy-done, bf16[4096,1024]{1,0:T(8,128)(2,1)} %constant.2.clone.table_ref), custom_call_target="tpu_custom_call" | custom-call | tf_op jit(solution)/shard_map/pallas_call | solution.py:208
  220.6 4.8 %copy.9 = f32[2,1,32,16,1024]{4,3,2,1,0:T(8,128)} copy(f32[2,1,32,16,1024]{4,3,2,1,0:T(8,128)} %bitcast.3) | data formatting | bytes 8388608
Async XLA Ops:
  0.9 1.9 copy-start

commit v2 on v1

v2 whole, which is shorter than its diff:
```python
import functools

import jax
import jax.numpy as jnp
import ml_dtypes
import numpy as np
from jax import lax
from jax.experimental import pallas as pl
from jax.experimental.pallas import tpu as pltpu
from jax.sharding import PartitionSpec as P

CH = 64
BLK = 3
NF = 2048
BAND = 128
BANDS = NF // BAND
NLAG = 1024
WIN = 8
PAIR = 32
SLOTS = 2
SRC = 32
RCV = 16
PIECES = 2 * BANDS
GROUP = 16
STAGES = [(0, 1), (0, 0), (1, 1), (1, 0)]
MESH = pl.DeviceIdType.MESH

whiten_eps = 1e-06


def lag_table():
    freqs = np.arange(NF, dtype=np.int64)
    offsets = np.arange(NLAG, dtype=np.int64) - NLAG // 2
    phases = np.mod(freqs[:, None] * np.abs(offsets)[None, :], 2 * NF)
    angles = phases.astype(np.float32) * np.float32(np.pi / NF)
    weights = np.where(freqs == 0, 1.0, 2.0).astype(np.float32) / np.sqrt(np.float32(NF * WIN))
    cos_table = weights[:, None] * np.cos(angles)
    sin_table = -weights[:, None] * (np.sign(offsets).astype(np.float32)[None, :] * np.sin(angles))
    return np.concatenate([cos_table, sin_table], axis=0).astype(ml_dtypes.bfloat16)


def peer_of(me, step):
    y = lax.rem(me // 8 + step // 8, 4)
    x = lax.rem(lax.rem(me // 2, 4) + lax.rem(step // 2, 4), 4)
    core = lax.rem(lax.rem(me, 2) + lax.rem(step, 2), 2)
    return (y * 4 + x) * 2 + core


def job_of(device, win):
    x, core = lax.rem(device // 2, 4), lax.rem(device, 2)
    return x // 2, lax.rem(lax.rem(x, 2) + 2 * core + win // 2, 4)


def kernel(
    list_ref, spec_ref, table_ref, out_ref,
    spec, white, blocks_0, blocks_1, outgoing, plane_in, job_in, src_wide, cross, table, result,
    spec_sem, table_sem, one_send, one_recv, z_send, z_recv, two_send, two_recv, back_send, back_recv,
):
    me = lax.axis_index("pair")
    win = lax.axis_index("win")
    row, column = me // 8, lax.rem(me, 8)

    spec_copy = pltpu.make_async_copy(spec_ref, spec, spec_sem)
    spec_copy.start()
    table_copy = pltpu.make_async_copy(table_ref, table, table_sem)
    table_copy.start()

    slot, quad = job_of(me, win)
    owner = row * 8 + win
    tiles = [quad * 2 + t for t in range(2)]
    own = [(owner == me) & (tile == win) for tile in tiles]
    shift = lax.rem(win // 2 - column // 2 + 4, 4)
    makers = [row * 8 + (2 * i + lax.rem(shift, 2)) * 2 + shift // 2 for i in range(SLOTS)]

    barrier = pltpu.get_barrier_semaphore()

    def greet(pair, plane):
        pl.semaphore_signal(barrier, inc=1, device_id=(pair, plane), device_id_type=MESH)

    def greet_pair(step, carry):
        greet(peer_of(me, step), win)
        return carry

    def greet_win(step, carry):
        greet(me, lax.rem(win + step, WIN))
        return carry

    lax.fori_loop(1, PAIR, greet_pair, 0)
    lax.fori_loop(1, WIN, greet_win, 0)
    count = PAIR - 1 + WIN - 1
    for t in range(2):
        here = own[t]

        @pl.when(jnp.logical_not(here))
        def _():
            greet(owner, tiles[t])

        count = count + jnp.where(here, 0, 1)
    for i in range(SLOTS):
        here = (makers[i] == me) & (column == win)

        @pl.when(jnp.logical_not(here))
        def _():
            greet(makers[i], column)

        count = count + jnp.where(here, 0, 1)

    all_blocks = (blocks_0, blocks_1)

    spec_copy.wait()

    def whiten(band, carry):
        cols = pl.ds(pl.multiple_of(band * BAND, BAND), BAND)
        re = spec[0, 0, :, cols]
        im = spec[1, 0, :, cols]
        level = jnp.sum(re * re + im * im, axis=-1, keepdims=True) * (1.0 / BAND)
        scale = lax.rsqrt(level + whiten_eps)
        for part, value in enumerate((re, im)):
            piece = (value * scale).astype(jnp.bfloat16).reshape(BLK, 2, 2, GROUP, BAND)
            for k in range(2):
                white[k, part * BANDS + band] = piece[:, :, k]
        return carry

    lax.fori_loop(0, BANDS, whiten, 0)

    pl.semaphore_wait(barrier, count)

    for k in range(2):
        def send_one(step, carry):
            to = peer_of(me, step)
            pltpu.make_async_remote_copy(
                src_ref=white.at[k, to],
                dst_ref=all_blocks[k].at[pl.ds(me * BLK, BLK)],
                send_sem=one_send.at[k],
                recv_sem=one_recv.at[k],
                device_id=(to, win),
                device_id_type=MESH,
            ).start()
            return carry

        lax.fori_loop(1, PAIR, send_one, 0)
        all_blocks[k][pl.ds(me * BLK, BLK)] = white[k, me]

    for stage, (k, role) in enumerate(STAGES):
        if stage % 2 == 0:
            most = all_blocks[k].at[pl.ds(0, (PAIR - 1) * BLK)]
            pltpu.make_async_copy(most, most, one_recv.at[k]).wait()

        def pick(plane):
            return [
                (o, i, all_blocks[k][list_ref[(o * 8 + plane) * 4 + i * 2 + role]])
                for o in range(4) for i in range(SLOTS)
            ]

        def send_z(step, carry):
            to = lax.rem(win + step, WIN)
            for o, i, block in pick(to):
                outgoing[stage, to, o, i] = block
            pltpu.make_async_remote_copy(
                src_ref=outgoing.at[stage, to],
                dst_ref=plane_in.at[stage, win],
                send_sem=z_send.at[stage],
                recv_sem=z_recv.at[stage],
                device_id=(me, to),
                device_id_type=MESH,
            ).start()
            return carry

        lax.fori_loop(1, WIN, send_z, 0)
        for o, i, block in pick(win):
            plane_in[stage, win, o, i] = block

    def spread(stage):
        k, role = STAGES[stage]
        most = plane_in.at[stage, pl.ds(0, WIN - 1)]
        pltpu.make_async_copy(most, most, z_recv.at[stage]).wait()

        def view(to):
            i, pair_of_tiles = job_of(to, win)
            half = pair_of_tiles // 2 if role == 0 else lax.rem(pair_of_tiles, 2)
            return plane_in.at[stage, :, to // 8, i, half]

        def send_two(step, carry):
            to = peer_of(me, step)
            pltpu.make_async_remote_copy(
                src_ref=view(to),
                dst_ref=job_in.at[stage, me],
                send_sem=two_send.at[stage],
                recv_sem=two_recv.at[stage],
                device_id=(to, win),
                device_id_type=MESH,
            ).start()
            return carry

        lax.fori_loop(1, PAIR, send_two, 0)
        job_in[stage, me] = view(me)[...]

    def arrived(stage):
        most = job_in.at[stage, pl.ds(0, PAIR - 1)]
        pltpu.make_async_copy(most, most, two_recv.at[stage]).wait()

    def work(half, t):
        src, rcv = job_in.at[STAGES.index((half, 0))], job_in.at[STAGES.index((t, 1))]
        unit = half * 2 + t

        def one_band(band, carry):
            receivers = []
            for w in range(WIN):
                for part in range(2):
                    src_wide[part, w] = src[part * BANDS + band, w].astype(jnp.float32)
                    receivers.append(rcv[part * BANDS + band, w].astype(jnp.float32))

            def one_source(a, inner):
                re = jnp.zeros((RCV, BAND), jnp.float32)
                im = jnp.zeros((RCV, BAND), jnp.float32)
                for w in range(WIN):
                    s_re = jnp.broadcast_to(src_wide[0, w, pl.ds(a, 1), :], (RCV, BAND))
                    s_im = jnp.broadcast_to(src_wide[1, w, pl.ds(a, 1), :], (RCV, BAND))
                    r_re, r_im = receivers[2 * w], receivers[2 * w + 1]
                    re = re + s_re * r_re + s_im * r_im
                    im = im + s_im * r_re - s_re * r_im
                rows = pl.ds(pl.multiple_of(a * RCV, RCV), RCV)
                cross[rows, pl.ds(pl.multiple_of(band * BAND, BAND), BAND)] = re.astype(jnp.bfloat16)
                cross[rows, pl.ds(pl.multiple_of(NF + band * BAND, BAND), BAND)] = im.astype(jnp.bfloat16)
                return inner

            lax.fori_loop(0, GROUP, one_source, 0)
            return carry

        lax.fori_loop(0, BANDS, one_band, 0)

        def one_tile(tile, carry):
            cols = pl.ds(pl.multiple_of(tile * 256, 256), 256)
            lags = jnp.dot(cross[...], table[:, cols], preferred_element_type=jnp.float32)
            result[unit, :, cols] = lags.astype(jnp.bfloat16)
            return carry

        lax.fori_loop(0, NLAG // 256, one_tile, 0)

        @pl.when(own[t])
        def _():
            pltpu.make_async_copy(result.at[unit], out_ref.at[slot, half], back_recv.at[slot, half]).start()

        @pl.when(jnp.logical_not(own[t]))
        def _():
            pltpu.make_async_remote_copy(
                src_ref=result.at[unit],
                dst_ref=out_ref.at[slot, half],
                send_sem=back_send.at[unit],
                recv_sem=back_recv.at[slot, half],
                device_id=(owner, tiles[t]),
                device_id_type=MESH,
            ).start()

    spread(0)
    spread(1)
    spread(2)
    table_copy.wait()
    arrived(0)
    arrived(1)
    work(0, 0)
    spread(3)
    arrived(2)
    work(0, 1)
    arrived(3)
    work(1, 0)
    work(1, 1)

    for k in range(2):
        sent = white.at[k, pl.ds(0, PAIR - 1)]
        pltpu.make_async_copy(sent, sent, one_send.at[k]).wait()
    for stage in range(4):
        sent = outgoing.at[stage, pl.ds(0, WIN - 1)]
        pltpu.make_async_copy(sent, sent, z_send.at[stage]).wait()
        sent = job_in.at[stage, pl.ds(0, PAIR - 1)]
        pltpu.make_async_copy(sent, sent, two_send.at[stage]).wait()
    for half in range(2):
        for t in range(2):
            sent = result.at[half * 2 + t]

            @pl.when(jnp.logical_not(own[t]))
            def _():
                pltpu.make_async_copy(sent, sent, back_send.at[half * 2 + t]).wait()

        for i in range(SLOTS):
            tile = out_ref.at[i, half]
            pltpu.make_async_copy(tile, tile, back_recv.at[i, half]).wait()


def body(spectra, pair_list):
    table = jnp.asarray(lag_table())
    rows = GROUP * RCV
    bf16 = jnp.bfloat16
    dma = pltpu.SemaphoreType.DMA
    out = pl.pallas_call(
        kernel,
        out_shape=jax.ShapeDtypeStruct((SLOTS, 2, rows, NLAG), bf16),
        in_specs=[
            pl.BlockSpec(memory_space=pltpu.SMEM),
            pl.BlockSpec(memory_space=pl.ANY),
            pl.BlockSpec(memory_space=pl.ANY),
        ],
        out_specs=pl.BlockSpec(memory_space=pl.ANY),
        scratch_shapes=[
            pltpu.VMEM((2, 1, BLK * CH, NF), jnp.float32),
            pltpu.VMEM((2, PIECES, BLK, 2, GROUP, BAND), bf16),
            pltpu.VMEM((PAIR * BLK, 2, GROUP, BAND), bf16),
            pltpu.VMEM((PAIR * BLK, 2, GROUP, BAND), bf16),
            pltpu.VMEM((4, WIN, 4, SLOTS, 2, GROUP, BAND), bf16),
            pltpu.VMEM((4, WIN, 4, SLOTS, 2, GROUP, BAND), bf16),
            pltpu.VMEM((4, PIECES, WIN, GROUP, BAND), bf16),
            pltpu.VMEM((2, WIN, GROUP, BAND), jnp.float32),
            pltpu.VMEM((rows, 2 * NF), bf16),
            pltpu.VMEM((2 * NF, NLAG), bf16),
            pltpu.VMEM((4, rows, NLAG), bf16),
            dma, dma,
            dma((2,)), dma((2,)),
            dma((4,)), dma((4,)),
            dma((4,)), dma((4,)),
            dma((4,)), dma((SLOTS, 2)),
        ],
        compiler_params=pltpu.CompilerParams(
            collective_id=0, has_side_effects=True, vmem_limit_bytes=48 * 1024 * 1024
        ),
    )(pair_list.reshape(-1), spectra, table)
    return out.astype(jnp.float32).reshape(SLOTS, 1, SRC, RCV, NLAG)


def solution(mesh):
    in_specs = (P(None, "win", "pair", None), P())
    out_specs = P("pair", "win", None, None, None)
    return jax.shard_map(body, mesh=mesh, in_specs=in_specs, out_specs=out_specs, check_vma=False)
```

time: 226 us -> 149 us (0.66)
  the two profiles are of different devices: /device:TPU:1 before, /device:TPU:120 now
where the time goes in v2:
time: 149 us
  Pallas kernels  144 us (97%)
  local copies, waits for them, and re-layouts  2.81 us (2%)
  other arithmetic  2.53 us (2%)
    pallas_call x1, Pallas kernels, body(): pl.pallas_call(kernel, out_shape=jax.ShapeDtypeStruct((SLOTS, 2, rows, NL...  144 us

profile of v2, /device:TPU:120, one launch (start us, length us, event | category | flops | bytes accessed | tf_op | source)
XLA Modules:
  0.0 149.0 jit_solution(5321630610933125513)
XLA Ops:
  0.0 0.8 copy.6
  0.8 0.1 reshape.9.list_ref
  0.9 0.0 copy-start
  0.9 1.9 %copy-done = f32[2,1,192,2048]{3,2,1,0:T(8,128)S(1)} copy-done((f32[2,1,192,2048]{3,2,1,0:T(8,128)S(1)}, f32[2,1,192,2048]{3,2,1,0:T(8,128)}, u32[]{:S(2)}) %copy-start) | copy-done | bytes 3145752
  2.8 143.7 %shard_map.37 = bf16[2,2,256,1024]{3,2,1,0:T(8,128)(2,1)S(1)} custom-call(s32[128]{0:T(128)S(1)} %reshape.9.list_ref, f32[2,1,192,2048]{3,2,1,0:T(8,128)S(1)} %copy-done, bf16[4096,1024]{1,0:T(8,128)(2,1)} %constant.2.clone.table_ref), custom_call_target="tpu_custom_call" | custom-call | tf_op jit(solution)/shard_map/pallas_call | solution.py:295
  146.5 2.5 %convert.2 = f32[2,1,32,16,1024]{4,3,2,1,0:T(8,128)} convert(bf16[2,1,32,16,1024]{4,3,2,1,0:T(8,128)(2,1)S(1)} %bitcast.5) | non-fusion elementwise | flops 1048576 | bytes 6291456 | tf_op jit(solution)/shard_map/reshape | solution.py:326
Async XLA Ops:
  0.9 1.9 %copy-start = (f32[2,1,192,2048]{3,2,1,0:T(8,128)S(1)}, f32[2,1,192,2048]{3,2,1,0:T(8,128)}, u32[]{:S(2)}) copy-start(f32[2,1,192,2048]{3,2,1,0:T(8,128)} %spec_ref.1) | copy-start | bytes 9437188

commit v3 on v2

v3 whole, which is shorter than its diff:
```python
import functools

import jax
import jax.numpy as jnp
import ml_dtypes
import numpy as np
from jax import lax
from jax.experimental import pallas as pl
from jax.experimental.pallas import tpu as pltpu
from jax.sharding import PartitionSpec as P

CH = 64
BLK = 3
NF = 2048
BAND = 128
BANDS = NF // BAND
NLAG = 1024
WIN = 8
PAIR = 32
SLOTS = 2
SRC = 32
RCV = 16
PIECES = 2 * BANDS
GROUP = 16
PART = 8
STAGES = [(0, 1), (0, 0), (1, 1), (1, 0)]
MESH = pl.DeviceIdType.MESH

whiten_eps = 1e-06


def lag_table():
    freqs = np.arange(NF, dtype=np.int64)
    offsets = np.arange(NLAG, dtype=np.int64) - NLAG // 2
    phases = np.mod(freqs[:, None] * np.abs(offsets)[None, :], 2 * NF)
    angles = phases.astype(np.float32) * np.float32(np.pi / NF)
    weights = np.where(freqs == 0, 1.0, 2.0).astype(np.float32) / np.sqrt(np.float32(NF * WIN))
    cos_table = weights[:, None] * np.cos(angles)
    sin_table = -weights[:, None] * (np.sign(offsets).astype(np.float32)[None, :] * np.sin(angles))
    return np.concatenate([cos_table, sin_table], axis=0).astype(ml_dtypes.bfloat16)


def peer_of(me, step):
    y = lax.rem(me // 8 + step // 8, 4)
    x = lax.rem(lax.rem(me // 2, 4) + lax.rem(step // 2, 4), 4)
    core = lax.rem(lax.rem(me, 2) + lax.rem(step, 2), 2)
    return (y * 4 + x) * 2 + core


def job_of(device, win):
    x, core = lax.rem(device // 2, 4), lax.rem(device, 2)
    return core, lax.rem(x + 2 * lax.rem(win + core, 2) + win // 2, 4)


def kernel(
    list_ref, spec_ref, table_ref, out_ref,
    spec, white, blocks_0, blocks_1, outgoing, plane_in, src_in, rcv_in, src_wide, cross, table, result,
    spec_sem, table_sem, one_send, one_recv, z_send, z_recv, two_send, two_recv, back_send, back_recv,
):
    me = lax.axis_index("pair")
    win = lax.axis_index("win")
    row, column = me // 8, lax.rem(me, 8)
    chip, core = me // 2, lax.rem(me, 2)

    spec_copy = pltpu.make_async_copy(spec_ref, spec, spec_sem)
    spec_copy.start()
    table_copy = pltpu.make_async_copy(table_ref, table, table_sem)
    table_copy.start()

    slot, quad = job_of(me, win)
    owner = row * 8 + win

    def is_own(t):
        return (owner == me) & (quad * 2 + t == win)

    shift = win // 2 - column // 2 + 4
    makers = [row * 8 + lax.rem(shift + 2 * lax.rem(column + i, 2), 4) * 2 + i for i in range(SLOTS)]

    barrier = pltpu.get_barrier_semaphore()

    def greet(pair, plane):
        pl.semaphore_signal(barrier, inc=1, device_id=(pair, plane), device_id_type=MESH)

    def greet_pair(step, carry):
        greet(peer_of(me, step), win)
        return carry

    def greet_win(step, carry):
        greet(me, lax.rem(win + step, WIN))
        return carry

    lax.fori_loop(1, PAIR, greet_pair, 0)
    lax.fori_loop(1, WIN, greet_win, 0)
    count = PAIR - 1 + WIN - 1
    for t in range(2):
        here = is_own(t)

        @pl.when(jnp.logical_not(here))
        def _():
            greet(owner, quad * 2 + t)

        count = count + jnp.where(here, 0, 1)
    for i in range(SLOTS):
        here = (makers[i] == me) & (column == win)

        @pl.when(jnp.logical_not(here))
        def _():
            greet(makers[i], column)

        count = count + jnp.where(here, 0, 1)

    all_blocks = (blocks_0, blocks_1)

    spec_copy.wait()

    def whiten(band, carry):
        cols = pl.ds(pl.multiple_of(band * BAND, BAND), BAND)
        re = spec[0, 0, :, cols]
        im = spec[1, 0, :, cols]
        level = jnp.sum(re * re + im * im, axis=-1, keepdims=True) * (1.0 / BAND)
        scale = lax.rsqrt(level + whiten_eps)
        for part, value in enumerate((re, im)):
            piece = (value * scale).astype(jnp.bfloat16).reshape(BLK, 2, 2, GROUP, BAND)
            for k in range(2):
                white[k, part * BANDS + band] = piece[:, :, k]
        return carry

    lax.fori_loop(0, BANDS, whiten, 0)

    pl.semaphore_wait(barrier, count)

    def one_copy(k, step):
        to = peer_of(me, step)
        return pltpu.make_async_remote_copy(
            src_ref=white.at[k, to],
            dst_ref=all_blocks[k].at[pl.ds(me * BLK, BLK)],
            send_sem=one_send.at[k, step],
            recv_sem=one_recv.at[k],
            device_id=(to, win),
            device_id_type=MESH,
        )

    def scatter(k):
        def send_one(step, carry):
            if k:
                one_copy(k - 1, step).wait_send()
            one_copy(k, step).start()
            return carry

        lax.fori_loop(1, PAIR, send_one, 0)
        all_blocks[k][pl.ds(me * BLK, BLK)] = white[k, me]

    def scatter_arrived(k):
        most = all_blocks[k].at[pl.ds(0, (PAIR - 1) * BLK)]
        pltpu.make_async_copy(most, most, one_recv.at[k]).wait()

    def pick(stage):
        i = stage // 4
        k, role = STAGES[stage % 4]

        def pick_for(step, carry):
            to = lax.rem(win + step, WIN)
            for o in range(4):
                outgoing[stage, to, o] = all_blocks[k][list_ref[(o * 8 + to) * 4 + i * 2 + role]]
            return carry

        lax.fori_loop(1, WIN, pick_for, 0)
        for o in range(4):
            plane_in[stage, win, o] = all_blocks[k][list_ref[(o * 8 + win) * 4 + i * 2 + role]]

    def z_copy(stage, step):
        to = lax.rem(win + step, WIN)
        return pltpu.make_async_remote_copy(
            src_ref=outgoing.at[stage, to],
            dst_ref=plane_in.at[stage, win],
            send_sem=z_send.at[stage, step],
            recv_sem=z_recv.at[stage],
            device_id=(me, to),
            device_id_type=MESH,
        )

    def send_planes(stage):
        def send_z(step, carry):
            if stage:
                z_copy(stage - 1, step).wait_send()
            z_copy(stage, step).start()
            return carry

        lax.fori_loop(1, WIN, send_z, 0)

    def spread(stage):
        i = stage // 4
        k, role = STAGES[stage % 4]
        most = plane_in.at[stage, pl.ds(0, WIN - 1)]
        pltpu.make_async_copy(most, most, z_recv.at[stage]).wait()
        dst = (rcv_in if role else src_in).at[k, me]

        def view(to):
            quad_there = job_of(to, win)[1]
            half = lax.rem(quad_there, 2) if role else quad_there // 2
            return plane_in.at[stage, :, to // 8, half]

        def send_two(step, carry):
            to = peer_of(me, step * 2 + lax.rem(core + i, 2))
            pltpu.make_async_remote_copy(
                src_ref=view(to),
                dst_ref=dst,
                send_sem=two_send.at[stage],
                recv_sem=two_recv.at[stage % 4],
                device_id=(to, win),
                device_id_type=MESH,
            ).start()
            return carry

        @pl.when(core == i)
        def _():
            dst[...] = view(me)[...]

        lax.fori_loop(jnp.where(core == i, 1, 0), PAIR // 2, send_two, 0)

    def arrived(j):
        k, role = STAGES[j]
        most = (rcv_in if role else src_in).at[k, pl.ds(0, PAIR - 1)]
        pltpu.make_async_copy(most, most, two_recv.at[j]).wait()

    def work(unit):
        half, t = unit // 2, unit % 2
        src, rcv = src_in.at[half], rcv_in.at[t]
        here = is_own(t)

        def one_part(e, carry):
            def one_band(band, inner):
                receivers = []
                for w in range(WIN):
                    s_re = src[band, w].astype(jnp.float32)
                    s_im = src[BANDS + band, w].astype(jnp.float32)
                    for n, value in enumerate((s_re, s_im, s_re + s_im)):
                        src_wide[n, w] = value
                    r_re = rcv[band, w].astype(jnp.float32)
                    r_im = rcv[BANDS + band, w].astype(jnp.float32)
                    receivers.append((r_re, r_re + r_im, r_re - r_im))

                for a in range(PART):
                    both = left = right = jnp.zeros((RCV, BAND), jnp.float32)
                    for w in range(WIN):
                        s_re, s_im, s_sum = (
                            jnp.broadcast_to(src_wide[n, w, pl.ds(e * PART + a, 1), :], (RCV, BAND)) for n in range(3)
                        )
                        r_re, r_sum, r_diff = receivers[w]
                        both = both + s_sum * r_re
                        left = left + s_re * r_sum
                        right = right + s_im * r_diff
                    rows = pl.ds(a * RCV, RCV)
                    cols = pl.multiple_of(band * BAND, BAND)
                    cross[rows, pl.ds(cols, BAND)] = (both - right).astype(jnp.bfloat16)
                    cross[rows, pl.ds(NF + cols, BAND)] = (both - left).astype(jnp.bfloat16)
                return inner

            lax.fori_loop(0, BANDS, one_band, 0)
            rows = pl.ds(pl.multiple_of(e * PART * RCV, PART * RCV), PART * RCV)

            def one_tile(tile, inner):
                cols = pl.ds(pl.multiple_of(tile * 512, 512), 512)
                lags = jnp.dot(cross[...], table[:, cols], preferred_element_type=jnp.float32)
                result[unit, rows, cols] = lags.astype(jnp.bfloat16)
                return inner

            lax.fori_loop(0, NLAG // 512, one_tile, 0)

            @pl.when(here)
            def _():
                pltpu.make_async_copy(
                    result.at[unit, rows], out_ref.at[slot, half, rows], back_recv.at[slot, half, e]
                ).start()

            @pl.when(jnp.logical_not(here))
            def _():
                pltpu.make_async_remote_copy(
                    src_ref=result.at[unit, rows],
                    dst_ref=out_ref.at[slot, half, rows],
                    send_sem=back_send.at[unit, e],
                    recv_sem=back_recv.at[slot, half, e],
                    device_id=(owner, quad * 2 + t),
                    device_id_type=MESH,
                ).start()

            return carry

        lax.fori_loop(0, GROUP // PART, one_part, 0)

    def work_after(i, unit, *stages):
        @pl.when(core == i)
        def _():
            for j in stages:
                arrived(j)
            work(unit)

    scatter(0)
    scatter(1)
    scatter_arrived(0)
    pick(0)
    send_planes(0)
    pick(1)
    send_planes(1)
    spread(0)
    scatter_arrived(1)
    pick(2)
    send_planes(2)
    pick(3)
    spread(1)
    send_planes(3)
    pick(4)
    spread(2)
    send_planes(4)
    pick(5)
    spread(3)
    send_planes(5)
    pick(6)
    pick(7)
    table_copy.wait()
    spread(4)
    send_planes(6)
    work_after(0, 0, 0, 1)
    spread(5)
    send_planes(7)
    work_after(0, 1, 2)
    spread(6)
    work_after(0, 2, 3)
    spread(7)
    work_after(0, 3)
    work_after(1, 0, 0, 1)
    work_after(1, 1, 2)
    work_after(1, 2, 3)
    work_after(1, 3)

    def last_sent(step, carry):
        one_copy(1, step).wait_send()
        return carry

    lax.fori_loop(1, PAIR, last_sent, 0)
    for step in range(1, WIN):
        z_copy(7, step).wait_send()
    for stage in range(8):
        for i in range(2):
            @pl.when(lax.rem(core + i, 2) == stage // 4)
            def _():
                sent = src_in.at[0, pl.ds(0, PAIR // 2 - 1 + i)]
                pltpu.make_async_copy(sent, sent, two_send.at[stage]).wait()

    for half in range(2):
        for e in range(GROUP // PART):
            rows = pl.ds(e * PART * RCV, PART * RCV)
            for t in range(2):
                sent = result.at[half * 2 + t, rows]

                @pl.when(jnp.logical_not(is_own(t)))
                def _():
                    pltpu.make_async_copy(sent, sent, back_send.at[half * 2 + t, e]).wait()

            for i in range(SLOTS):
                tile = out_ref.at[i, half, rows]
                pltpu.make_async_copy(tile, tile, back_recv.at[i, half, e]).wait()


def body(spectra, pair_list):
    table = jnp.asarray(lag_table())
    rows = GROUP * RCV
    bf16 = jnp.bfloat16
    dma = pltpu.SemaphoreType.DMA
    out = pl.pallas_call(
        kernel,
        out_shape=jax.ShapeDtypeStruct((SLOTS, 2, rows, NLAG), bf16),
        in_specs=[
            pl.BlockSpec(memory_space=pltpu.SMEM),
            pl.BlockSpec(memory_space=pl.ANY),
            pl.BlockSpec(memory_space=pl.ANY),
        ],
        out_specs=pl.BlockSpec(memory_space=pl.ANY),
        scratch_shapes=[
            pltpu.VMEM((2, 1, BLK * CH, NF), jnp.float32),
            pltpu.VMEM((2, PIECES, BLK, 2, GROUP, BAND), bf16),
            pltpu.VMEM((PAIR * BLK, 2, GROUP, BAND), bf16),
            pltpu.VMEM((PAIR * BLK, 2, GROUP, BAND), bf16),
            pltpu.VMEM((8, WIN, 4, 2, GROUP, BAND), bf16),
            pltpu.VMEM((8, WIN, 4, 2, GROUP, BAND), bf16),
            pltpu.VMEM((2, PIECES, WIN, GROUP, BAND), bf16),
            pltpu.VMEM((2, PIECES, WIN, GROUP, BAND), bf16),
            pltpu.VMEM((3, WIN, GROUP, BAND), jnp.float32),
            pltpu.VMEM((PART * RCV, 2 * NF), bf16),
            pltpu.VMEM((2 * NF, NLAG), bf16),
            pltpu.VMEM((4, rows, NLAG), bf16),
            dma, dma,
            dma((2, PAIR)), dma((2,)),
            dma((8, WIN)), dma((8,)),
            dma((8,)), dma((4,)),
            dma((4, GROUP // PART)), dma((SLOTS, 2, GROUP // PART)),
        ],
        compiler_params=pltpu.CompilerParams(
            collective_id=0, has_side_effects=True, vmem_limit_bytes=60 * 1024 * 1024
        ),
    )(pair_list.reshape(-1), spectra, table)
    return out.astype(jnp.float32).reshape(SLOTS, 1, SRC, RCV, NLAG)


def solution(mesh):
    in_specs = (P(None, "win", "pair", None), P())
    out_specs = P("pair", "win", None, None, None)
    return jax.shard_map(body, mesh=mesh, in_specs=in_specs, out_specs=out_specs, check_vma=False)
```

time: 149 us -> 135 us (0.906)
  the two profiles are of different devices: /device:TPU:120 before, /device:TPU:162 now
where the time goes in v3:
time: 135 us
  Pallas kernels  130 us (96%)
  other arithmetic  4.11 us (3%)
  local copies, waits for them, and re-layouts  1.44 us (1%)
    pallas_call x1, Pallas kernels, body(): pl.pallas_call(kernel, out_shape=jax.ShapeDtypeStruct((SLOTS, 2, rows, NL...  130 us
    reshape x1, other arithmetic, body(): return out.astype(jnp.float32).reshape(SLOTS, 1, SRC, RCV, NLAG)  4.11 us

profile of v3, /device:TPU:162, one launch (start us, length us, event | category | flops | bytes accessed | tf_op | source)
XLA Modules:
  0.0 135.2 jit_solution(13406773895256032025)
XLA Ops:
  0.0 0.8 copy.6
  0.8 0.7 reshape.9.list_ref
  1.4 129.7 %shard_map.37 = bf16[2,2,256,1024]{3,2,1,0:T(8,128)(2,1)} custom-call(s32[128]{0:T(128)} %reshape.9.list_ref, f32[2,1,192,2048]{3,2,1,0:T(8,128)} %spec_ref.1, bf16[4096,1024]{1,0:T(8,128)(2,1)} %constant.2.clone.table_ref), custom_call_target="tpu_custom_call" | custom-call | tf_op jit(solution)/shard_map/pallas_call | solution.py:370
  131.1 4.1 %convert.2 = f32[2,1,32,16,1024]{4,3,2,1,0:T(8,128)} convert(bf16[2,1,32,16,1024]{4,3,2,1,0:T(8,128)(2,1)} %bitcast.5) | non-fusion elementwise | flops 1048576 | bytes 6291456 | tf_op jit(solution)/shard_map/reshape | solution.py:402

commit v4 on v3

--- a/solution.py
+++ b/solution.py
@@ -24,6 +24,7 @@
 GROUP = 16
 PART = 8
 STAGES = [(0, 1), (0, 0), (1, 1), (1, 0)]
+SENDS = [(0, (0,)), (1, (0,)), (0, (1,)), (1, (1,))] + [(stage, (0, 1)) for stage in range(2, 8)]
 MESH = pl.DeviceIdType.MESH
 
 whiten_eps = 1e-06
@@ -54,7 +55,7 @@
 
 def kernel(
     list_ref, spec_ref, table_ref, out_ref,
-    spec, white, blocks_0, blocks_1, outgoing, plane_in, src_in, rcv_in, src_wide, cross, table, result,
+    spec, white, blocks_0, blocks_1, blocks_2, blocks_3, outgoing, plane_in, src_in, rcv_in, src_wide, cross, table, result,
     spec_sem, table_sem, one_send, one_recv, z_send, z_recv, two_send, two_recv, back_send, back_recv,
 ):
     me = lax.axis_index("pair")
@@ -109,7 +110,7 @@
 
         count = count + jnp.where(here, 0, 1)
 
-    all_blocks = (blocks_0, blocks_1)
+    all_blocks = (blocks_0, blocks_1, blocks_2, blocks_3)
 
     spec_copy.wait()
 
@@ -122,77 +123,91 @@
         for part, value in enumerate((re, im)):
             piece = (value * scale).astype(jnp.bfloat16).reshape(BLK, 2, 2, GROUP, BAND)
             for k in range(2):
-                white[k, part * BANDS + band] = piece[:, :, k]
+                for h in range(2):
+                    white[k * 2 + h, part * BANDS + band] = piece[:, h, k]
         return carry
 
     lax.fori_loop(0, BANDS, whiten, 0)
 
     pl.semaphore_wait(barrier, count)
 
-    def one_copy(k, step):
+    def one_copy(part, step):
         to = peer_of(me, step)
         return pltpu.make_async_remote_copy(
-            src_ref=white.at[k, to],
-            dst_ref=all_blocks[k].at[pl.ds(me * BLK, BLK)],
-            send_sem=one_send.at[k, step],
-            recv_sem=one_recv.at[k],
+            src_ref=white.at[part, to],
+            dst_ref=all_blocks[part].at[pl.ds(me * BLK, BLK)],
+            send_sem=one_send.at[part, step],
+            recv_sem=one_recv.at[part],
             device_id=(to, win),
             device_id_type=MESH,
         )
 
-    def scatter(k):
+    def scatter(part):
         def send_one(step, carry):
-            if k:
-                one_copy(k - 1, step).wait_send()
-            one_copy(k, step).start()
+            one_copy(part, step).start()
             return carry
 
         lax.fori_loop(1, PAIR, send_one, 0)
-        all_blocks[k][pl.ds(me * BLK, BLK)] = white[k, me]
-
-    def scatter_arrived(k):
-        most = all_blocks[k].at[pl.ds(0, (PAIR - 1) * BLK)]
-        pltpu.make_async_copy(most, most, one_recv.at[k]).wait()
-
-    def pick(stage):
+        all_blocks[part][pl.ds(me * BLK, BLK)] = white[part, me]
+
+    def scatter_arrived(part):
+        most = all_blocks[part].at[pl.ds(0, (PAIR - 1) * BLK)]
+        pltpu.make_async_copy(most, most, one_recv.at[part]).wait()
+
+    def pick(n):
+        stage, halves = SENDS[n]
         i = stage // 4
         k, role = STAGES[stage % 4]
 
         def pick_for(step, carry):
-            to = lax.rem(win + step, WIN)
+            to = z_peer(step)
             for o in range(4):
-                outgoing[stage, to, o] = all_blocks[k][list_ref[(o * 8 + to) * 4 + i * 2 + role]]
+                for h in halves:
+                    outgoing[stage, to, o, h] = all_blocks[k * 2 + h][list_ref[i, role, o * 8 + to]]
             return carry
 
         lax.fori_loop(1, WIN, pick_for, 0)
         for o in range(4):
-            plane_in[stage, win, o] = all_blocks[k][list_ref[(o * 8 + win) * 4 + i * 2 + role]]
-
-    def z_copy(stage, step):
-        to = lax.rem(win + step, WIN)
+            for h in halves:
+                plane_in[stage, win, o, h] = all_blocks[k * 2 + h][list_ref[i, role, o * 8 + win]]
+
+    def z_peer(step):
+        return lax.rem(win + 4 + step // 2 * (2 * lax.rem(step, 2) - 1), WIN)
+
+    def z_copy(n, step):
+        stage, halves = SENDS[n]
+        to = z_peer(step)
+        whole = len(halves) == 2
         return pltpu.make_async_remote_copy(
-            src_ref=outgoing.at[stage, to],
-            dst_ref=plane_in.at[stage, win],
-            send_sem=z_send.at[stage, step],
-            recv_sem=z_recv.at[stage],
+            src_ref=outgoing.at[stage, to] if whole else outgoing.at[stage, to, :, halves[0]],
+            dst_ref=plane_in.at[stage, win] if whole else plane_in.at[stage, win, :, halves[0]],
+            send_sem=z_send.at[n, step],
+            recv_sem=z_recv.at[n],
             device_id=(me, to),
             device_id_type=MESH,
         )
 
-    def send_planes(stage):
+    def send_planes(n):
         def send_z(step, carry):
-            if stage:
-                z_copy(stage - 1, step).wait_send()
-            z_copy(stage, step).start()
+            for before in range(4) if n == 4 else range(n - 1, n) if n > 4 else ():
+                z_copy(before, step).wait_send()
+            z_copy(n, step).start()
             return carry
 
         lax.fori_loop(1, WIN, send_z, 0)
+
+    def planes_arrived(stage):
+        for n, (of, halves) in enumerate(SENDS):
+            if of == stage:
+                most = plane_in.at[stage, pl.ds(0, WIN - 1)]
+                if len(halves) == 1:
+                    most = plane_in.at[stage, pl.ds(0, WIN - 1), :, halves[0]]
+                pltpu.make_async_copy(most, most, z_recv.at[n]).wait()
 
     def spread(stage):
         i = stage // 4
         k, role = STAGES[stage % 4]
-        most = plane_in.at[stage, pl.ds(0, WIN - 1)]
-        pltpu.make_async_copy(most, most, z_recv.at[stage]).wait()
+        planes_arrived(stage)
         dst = (rcv_in if role else src_in).at[k, me]
 
         def view(to):
@@ -201,7 +216,7 @@
             return plane_in.at[stage, :, to // 8, half]
 
         def send_two(step, carry):
-            to = peer_of(me, step * 2 + lax.rem(core + i, 2))
+            to = peer_of(me, lax.rem(step * 7, PAIR // 2) * 2 + lax.rem(core + i, 2))
             pltpu.make_async_remote_copy(
                 src_ref=view(to),
                 dst_ref=dst,
@@ -302,27 +317,35 @@
     send_planes(0)
     pick(1)
     send_planes(1)
-    spread(0)
+    scatter(2)
     scatter_arrived(1)
     pick(2)
     send_planes(2)
     pick(3)
-    spread(1)
     send_planes(3)
+    scatter(3)
+    spread(0)
+    scatter_arrived(2)
+    scatter_arrived(3)
     pick(4)
-    spread(2)
     send_planes(4)
     pick(5)
-    spread(3)
+    spread(1)
     send_planes(5)
     pick(6)
+    spread(2)
+    send_planes(6)
     pick(7)
+    spread(3)
+    send_planes(7)
+    pick(8)
+    pick(9)
     table_copy.wait()
     spread(4)
-    send_planes(6)
+    send_planes(8)
     work_after(0, 0, 0, 1)
     spread(5)
-    send_planes(7)
+    send_planes(9)
     work_after(0, 1, 2)
     spread(6)
     work_after(0, 2, 3)
@@ -334,12 +357,13 @@
     work_after(1, 3)
 
     def last_sent(step, carry):
-        one_copy(1, step).wait_send()
+        for part in range(4):
+            one_copy(part, step).wait_send()
         return carry
 
     lax.fori_loop(1, PAIR, last_sent, 0)
     for step in range(1, WIN):
-        z_copy(7, step).wait_send()
+        z_copy(9, step).wait_send()
     for stage in range(8):
         for i in range(2):
             @pl.when(lax.rem(core + i, 2) == stage // 4)
@@ -378,9 +402,11 @@
         out_specs=pl.BlockSpec(memory_space=pl.ANY),
         scratch_shapes=[
             pltpu.VMEM((2, 1, BLK * CH, NF), jnp.float32),
-            pltpu.VMEM((2, PIECES, BLK, 2, GROUP, BAND), bf16),
-            pltpu.VMEM((PAIR * BLK, 2, GROUP, BAND), bf16),
-            pltpu.VMEM((PAIR * BLK, 2, GROUP, BAND), bf16),
+            pltpu.VMEM((4, PIECES, BLK, GROUP, BAND), bf16),
+            pltpu.VMEM((PAIR * BLK, GROUP, BAND), bf16),
+            pltpu.VMEM((PAIR * BLK, GROUP, BAND), bf16),
+            pltpu.VMEM((PAIR * BLK, GROUP, BAND), bf16),
+            pltpu.VMEM((PAIR * BLK, GROUP, BAND), bf16),
             pltpu.VMEM((8, WIN, 4, 2, GROUP, BAND), bf16),
             pltpu.VMEM((8, WIN, 4, 2, GROUP, BAND), bf16),
             pltpu.VMEM((2, PIECES, WIN, GROUP, BAND), bf16),
@@ -390,15 +416,15 @@
             pltpu.VMEM((2 * NF, NLAG), bf16),
             pltpu.VMEM((4, rows, NLAG), bf16),
             dma, dma,
-            dma((2, PAIR)), dma((2,)),
-            dma((8, WIN)), dma((8,)),
+            dma((4, PAIR)), dma((4,)),
+            dma((10, WIN)), dma((10,)),
             dma((8,)), dma((4,)),
             dma((4, GROUP // PART)), dma((SLOTS, 2, GROUP // PART)),
         ],
         compiler_params=pltpu.CompilerParams(
             collective_id=0, has_side_effects=True, vmem_limit_bytes=60 * 1024 * 1024
         ),
-    )(pair_list.reshape(-1), spectra, table)
+    )(pair_list.transpose(1, 2, 0), spectra, table)
     return out.astype(jnp.float32).reshape(SLOTS, 1, SRC, RCV, NLAG)
 
 

time: 135 us -> 131 us (0.970)
  Pallas kernels: 130 us -> 127 us
  local copies, waits for them, and re-layouts: 1.44 us -> 0 us
    pallas_call x1, Pallas kernels: 130 us -> 127 us  [body(): pl.pallas_call(kernel, out_shape=jax.ShapeDtypeStruct((SLOTS, 2, rows, NL...]
where the time goes in v4:
time: 131 us
  Pallas kernels  127 us (97%)
  other arithmetic  4.11 us (3%)
    pallas_call x1, Pallas kernels, body(): pl.pallas_call(kernel, out_shape=jax.ShapeDtypeStruct((SLOTS, 2, rows, NL...  127 us
    reshape x1, other arithmetic, body(): return out.astype(jnp.float32).reshape(SLOTS, 1, SRC, RCV, NLAG)  4.11 us

profile of v4, /device:TPU:162, one launch (start us, length us, event | category | flops | bytes accessed | tf_op | source)
XLA Modules:
  0.0 131.2 jit_solution(7359524108156157720)
XLA Ops:
  0.0 127.1 %shard_map.37 = bf16[2,2,256,1024]{3,2,1,0:T(8,128)(2,1)} custom-call(s32[2,2,32]{2,1,0:T(2,128)} %bitcast.7, f32[2,1,192,2048]{3,2,1,0:T(8,128)} %spec_ref.1, bf16[4096,1024]{1,0:T(8,128)(2,1)} %constant.2.clone.table_ref), custom_call_target="tpu_custom_call" | custom-call | tf_op jit(solution)/shard_map/pallas_call | solution.py:394
  127.1 4.1 %convert.2 = f32[2,1,32,16,1024]{4,3,2,1,0:T(8,128)} convert(bf16[2,1,32,16,1024]{4,3,2,1,0:T(8,128)(2,1)} %bitcast.6) | non-fusion elementwise | flops 1048576 | bytes 6291456 | tf_op jit(solution)/shard_map/reshape | solution.py:428

commit v5 on v4

--- a/solution.py
+++ b/solution.py
@@ -63,8 +63,13 @@
     row, column = me // 8, lax.rem(me, 8)
     chip, core = me // 2, lax.rem(me, 2)
 
-    spec_copy = pltpu.make_async_copy(spec_ref, spec, spec_sem)
-    spec_copy.start()
+    spec_copies = []
+    for n in range(4):
+        lanes = pl.ds(n * NF // 4, NF // 4)
+        spec_copies.append(
+            pltpu.make_async_copy(spec_ref.at[:, :, :, lanes], spec.at[:, :, :, lanes], spec_sem.at[n])
+        )
+        spec_copies[n].start()
     table_copy = pltpu.make_async_copy(table_ref, table, table_sem)
     table_copy.start()
 
@@ -111,8 +116,6 @@
         count = count + jnp.where(here, 0, 1)
 
     all_blocks = (blocks_0, blocks_1, blocks_2, blocks_3)
-
-    spec_copy.wait()
 
     def whiten(band, carry):
         cols = pl.ds(pl.multiple_of(band * BAND, BAND), BAND)
@@ -127,7 +130,9 @@
                     white[k * 2 + h, part * BANDS + band] = piece[:, h, k]
         return carry
 
-    lax.fori_loop(0, BANDS, whiten, 0)
+    for n in range(4):
+        spec_copies[n].wait()
+        lax.fori_loop(n * BANDS // 4, (n + 1) * BANDS // 4, whiten, 0)
 
     pl.semaphore_wait(barrier, count)
 
@@ -415,7 +420,7 @@
             pltpu.VMEM((PART * RCV, 2 * NF), bf16),
             pltpu.VMEM((2 * NF, NLAG), bf16),
             pltpu.VMEM((4, rows, NLAG), bf16),
-            dma, dma,
+            dma((4,)), dma,
             dma((4, PAIR)), dma((4,)),
             dma((10, WIN)), dma((10,)),
             dma((8,)), dma((4,)),

time: 131 us -> 132 us (level)
  no operation moved by 1% of the time
where the time goes in v5:
time: 132 us; the launch traced here: 131 us
  Pallas kernels  127 us (96%)
  other arithmetic  4.11 us (3%)
    pallas_call x1, Pallas kernels, body(): pl.pallas_call(kernel, out_shape=jax.ShapeDtypeStruct((SLOTS, 2, rows, NL...  127 us
    reshape x1, other arithmetic, body(): return out.astype(jnp.float32).reshape(SLOTS, 1, SRC, RCV, NLAG)  4.11 us

profile of v5, /device:TPU:162, one launch (start us, length us, event | category | flops | bytes accessed | tf_op | source)
XLA Modules:
  0.0 131.5 jit_solution(5755107524545061645)
XLA Ops:
  0.0 127.4 %shard_map.37 = bf16[2,2,256,1024]{3,2,1,0:T(8,128)(2,1)} custom-call(s32[2,2,32]{2,1,0:T(2,128)} %bitcast.7, f32[2,1,192,2048]{3,2,1,0:T(8,128)} %spec_ref.1, bf16[4096,1024]{1,0:T(8,128)(2,1)} %constant.2.clone.table_ref), custom_call_target="tpu_custom_call" | custom-call | tf_op jit(solution)/shard_map/pallas_call | solution.py:399
  127.4 4.1 %convert.2 = f32[2,1,32,16,1024]{4,3,2,1,0:T(8,128)} convert(bf16[2,1,32,16,1024]{4,3,2,1,0:T(8,128)(2,1)} %bitcast.6) | non-fusion elementwise | flops 1048576 | bytes 6291456 | tf_op jit(solution)/shard_map/reshape | solution.py:433
